TPU v7x, 512 devices: a whole 4x4x16 slice. The times are simulated.
512 devices in a mesh: node: 16 (over x, z_hi), local: 8 (over y, core), edata: 4 (over z_lo).
Axes of the slice: x: 4, y: 4, z: 16 (z_hi: 4, z_lo: 4; z = z_hi * 4 + z_lo), core: 2. Of those that a mesh axis runs over, the one named last changes fastest.
Arguments:
- tokens: bfloat16 [32768, 4096], P(('node', 'local'), 'edata'), may hold values from -6 to 6
- grad_out: bfloat16 [32768, 4096], P(('node', 'local'), 'edata'), may hold values from -0.59765625 to 0.59765625
- routes: int32 [32768, 2], P(('node', 'local')), may hold values from 0 to 63, all different within a row
- gates: bfloat16 [32768, 2], P(('node', 'local')), may hold values from 0.099609375 to 1
- w_in: bfloat16 [4096, 32768], P('edata', ('node', 'local')), may hold values from -0.09375 to 0.09375
- w_out: bfloat16 [32768, 4096], P(('node', 'local'), 'edata'), may hold values from -0.09375 to 0.09375
Outputs:
- grad_tokens: bfloat16 [32768, 4096], P(('node', 'local'), 'edata')
- grad_gates: float32 [32768, 2], P(('node', 'local'))
- grad_w_in: float32 [4096, 32768], P('edata', ('node', 'local'))
- grad_w_out: float32 [32768, 4096], P(('node', 'local'), 'edata')
Inputs may be any that keep to these rules, and one draw needn't show every extreme that they name: `routes`: each token names two different experts.
All inputs are finite; a program needn't handle non-finite values.
Results may differ from a plain program's by a relative error of at most 0.0049.
Values may be sent and summed in bfloat16 or wider, within the bound.
A program may use at most 64 MiB of HBM per device.

v0:
```python
import jax
import jax.numpy as jnp
from jax import lax
from jax.sharding import PartitionSpec as P

EXPERTS = 64
WINDOW = 2


def gelu_pair(pre_act):
    coefficient = 0.7978845608028654
    inner_arg = coefficient * (pre_act + 0.044715 * pre_act * pre_act * pre_act)
    tanh_val = jnp.tanh(inner_arg)
    activation = 0.5 * pre_act * (1.0 + tanh_val)
    slopes = 0.5 * (1.0 + tanh_val) + 0.5 * pre_act * (1.0 - tanh_val * tanh_val) * coefficient * (
        1.0 + 3.0 * 0.044715 * pre_act * pre_act
    )
    return (activation, slopes)


def body(tokens, grad_out, routes, gates, w_in, w_out):
    n_node = lax.axis_size("node")
    n_local = lax.axis_size("local")
    groups = n_node * n_local
    half_nodes = n_node // WINDOW
    tok_rows = tokens.shape[0]
    shard_cols = tokens.shape[1]
    capacity = 2 * tok_rows // EXPERTS
    slots = WINDOW * capacity
    flat_routes = routes.reshape(-1)
    in_window = (flat_routes[:, None] == jnp.arange(WINDOW, dtype=jnp.int32)[None, :]).astype(
        jnp.int32
    )
    before = jnp.cumsum(in_window, axis=0) - in_window
    position = jnp.sum(before * in_window, axis=1)
    live_pair = (flat_routes < WINDOW) & (position < capacity)
    slot_index = jnp.where(live_pair, flat_routes * capacity + position, -1)
    matches = slot_index[:, None] == jnp.arange(slots, dtype=jnp.int32)[None, :]
    placing = jnp.any(matches.reshape(tok_rows, 2, slots), axis=1).astype(jnp.bfloat16).T
    send_x = jnp.dot(placing, tokens, preferred_element_type=jnp.float32).astype(jnp.bfloat16)
    send_dy = jnp.dot(placing, grad_out, preferred_element_type=jnp.float32).astype(jnp.bfloat16)
    gate_flat = gates.reshape(-1)
    send_gate = jnp.sum(jnp.where(matches, gate_flat[:, None], jnp.zeros((), gates.dtype)), axis=0)
    spread_x = jnp.repeat(send_x.reshape(WINDOW, capacity, shard_cols), half_nodes, axis=0)
    spread_dy = jnp.repeat(send_dy.reshape(WINDOW, capacity, shard_cols), half_nodes, axis=0)
    spread_gate = jnp.repeat(send_gate.reshape(WINDOW, capacity), half_nodes, axis=0)
    got_x, got_dy, got_gate = (
        lax.all_to_all(spread_x, "node", split_axis=0, concat_axis=0, tiled=True),
        lax.all_to_all(spread_dy, "node", split_axis=0, concat_axis=0, tiled=True),
        lax.all_to_all(spread_gate, "node", split_axis=0, concat_axis=0, tiled=True),
    )
    rows_x, rows_dy, rows_gate = (
        lax.all_gather(got_x[:, None], "local", axis=1, tiled=True),
        lax.all_gather(got_dy[:, None], "local", axis=1, tiled=True),
        lax.all_gather(got_gate[:, None], "local", axis=1, tiled=True),
    )
    total_rows = groups * capacity
    x_rows = rows_x.reshape(total_rows, shard_cols)
    dy_rows = rows_dy.reshape(total_rows, shard_cols)
    gate_col = rows_gate.reshape(total_rows).astype(jnp.float32)[:, None]
    pre_part = jnp.dot(x_rows, w_in, preferred_element_type=jnp.float32)
    back_part = lax.dot_general(
        dy_rows, w_out, (((1,), (1,)), ((), ())), preferred_element_type=jnp.float32
    )
    pre_act, back_grad = lax.psum((pre_part, back_part), "edata")
    activation, slopes = gelu_pair(pre_act)
    scaled = (gate_col * activation).astype(jnp.bfloat16)
    grad_w_out = lax.dot_general(
        scaled, dy_rows, (((0,), (0,)), ((), ())), preferred_element_type=jnp.float32
    )
    pre_grad = (gate_col * back_grad * slopes).astype(jnp.bfloat16)
    grad_w_in = lax.dot_general(
        x_rows, pre_grad, (((0,), (0,)), ((), ())), preferred_element_type=jnp.float32
    )
    token_part = lax.dot_general(
        pre_grad, w_in, (((1,), (1,)), ((), ())), preferred_element_type=jnp.float32
    )
    gate_part = jnp.sum(activation * back_grad, axis=1)
    token_part = token_part.reshape(n_node, n_local, capacity, shard_cols)
    gate_part = gate_part.reshape(n_node, n_local, capacity)
    reduced_x, reduced_gate = (
        lax.psum_scatter(token_part, "local", scatter_dimension=1, tiled=True),
        lax.psum_scatter(gate_part, "local", scatter_dimension=1, tiled=True),
    )
    came_x, came_gate = (
        lax.all_to_all(reduced_x, "node", split_axis=0, concat_axis=0, tiled=True),
        lax.all_to_all(reduced_gate, "node", split_axis=0, concat_axis=0, tiled=True),
    )
    slot_grad = jnp.sum(came_x.reshape(WINDOW, half_nodes, capacity, shard_cols), axis=1)
    slot_gate = jnp.sum(came_gate.reshape(WINDOW, half_nodes, capacity), axis=1)
    slot_grad = slot_grad.reshape(slots, shard_cols)
    slot_gate = slot_gate.reshape(slots)
    safe_index = jnp.maximum(slot_index, 0)
    picked = slot_grad[safe_index].reshape(tok_rows, 2, shard_cols)
    keep_pair = live_pair.reshape(tok_rows, 2)
    grad_tokens = jnp.sum(
        jnp.where(keep_pair[:, :, None], picked, jnp.zeros((), jnp.float32)), axis=1
    ).astype(jnp.bfloat16)
    grad_gates = jnp.where(
        keep_pair, slot_gate[safe_index].reshape(tok_rows, 2), jnp.zeros((), jnp.float32)
    )
    return (grad_tokens, grad_gates, grad_w_in, grad_w_out)


def solution(mesh):
    in_specs = (
        P(("node", "local"), "edata"),
        P(("node", "local"), "edata"),
        P(("node", "local"), None),
        P(("node", "local"), None),
        P("edata", ("node", "local")),
        P(("node", "local"), "edata"),
    )
    out_specs = (
        P(("node", "local"), "edata"),
        P(("node", "local"), None),
        P("edata", ("node", "local")),
        P(("node", "local"), "edata"),
    )
    return jax.shard_map(body, mesh=mesh, in_specs=in_specs, out_specs=out_specs, check_vma=False)
```

profile of v0, /device:TPU:1, one launch (start us, length us, event | category | flops | bytes accessed | tf_op | source)
XLA Modules:
  0.0 377.7 jit_solution(12268287302546318466)
XLA Ops:
  7.2 0.9 copy.48
  8.4 0.6 reduce-window.6
  9.9 1.2 fusion.1
  11.1 38.0 %all_to_all.29 = bf16[16,8,1024]{2,1,0:T(8,128)(2,1)} all-to-all(bf16[16,8,1024]{2,1,0:T(8,128)(2,1)S(1)} %bitcast.74), channel_id=1, replica_groups=mesh['node'=16,'local'=8,'edata'=4] {'node'}, dimensions={0} | all-to-all | bytes 524288 | tf_op jit(solution)/shard_map/all_to_all | solution.py:48
  49.4 21.9 %all_to_all.30 = bf16[16,8,1024]{2,1,0:T(8,128)(2,1)} all-to-all(bf16[16,8,1024]{2,1,0:T(8,128)(2,1)S(1)} %bitcast.75), channel_id=1, replica_groups=mesh['node'=16,'local'=8,'edata'=4] {'node'}, dimensions={0} | all-to-all | bytes 524288 | tf_op jit(solution)/shard_map/all_to_all | solution.py:49
  71.3 5.3 %all-gather.7.cloned.1.call-done = bf16[16,64,1024]{2,1,0:T(8,128)(2,1)} async-done(((bf16[16,8,1024]{2,1,0:T(8,128)(2,1)}), bf16[16,64,1024]{2,1,0:T(8,128)(2,1)}) %all-gather.7.cloned.1.call-update) | async-done | bytes 2097168 | tf_op jit(solution)/shard_map/all_gather | solution.py:53
  76.6 3.3 fusion.25
  79.9 32.0 %all-gather.5.cloned.1.call-done = bf16[16,64,1024]{2,1,0:T(8,128)(2,1)} async-done(((bf16[16,8,1024]{2,1,0:T(8,128)(2,1)}), bf16[16,64,1024]{2,1,0:T(8,128)(2,1)}) %all-gather.5.cloned.1.call-update) | async-done | bytes 2097168 | tf_op jit(solution)/shard_map/all_gather | solution.py:54
  112.0 3.3 fusion.24
  115.3 0.6 copy-done.3
  116.8 27.8 %all_to_all.31 = bf16[16,1,8]{2,1,0:T(2,128)(2,1)S(1)} all-to-all(bf16[16,1,8]{2,1,0:T(2,128)(2,1)S(1)} %copy.53), channel_id=1, replica_groups=mesh['node'=16,'local'=8,'edata'=4] {'node'}, dimensions={0} | all-to-all | bytes 512 | tf_op jit(solution)/shard_map/all_to_all | solution.py:50
  144.7 12.7 %all_gather.9 = bf16[16,8,8]{0,2,1:T(8,128)(2,1)S(1)} all-gather(bf16[16,1,8]{0,2,1:T(8,128)(2,1)S(1)} %copy.54), channel_id=1, replica_groups=mesh['node'=16,'local'=8,'edata'=4] {'local'}, dimensions={1}, use_global_device_ids=true | all-gather | bytes 2304 | tf_op jit(solution)/shard_map/all_gather | solution.py:55
  157.6 66.3 %all-reduce.8.cloned.1.call-done = (f32[1024,256]{1,0:T(8,128)}, f32[1024,256]{1,0:T(8,128)}) async-done(((f32[1024,256]{1,0:T(8,128)}, f32[1024,256]{1,0:T(8,128)}), (f32[1024,256]{1,0:T(8,128)}, f32[1024,256]{1,0:T(8,128)})) %all-reduce.8.cloned.1.call-update) | async-done | bytes 2097168 | tf_op jit(solution)/shard_map/psum | solution.py:65
  224.0 2.6 multiply_reduce_fusion
  226.6 2.7 fusion.26
  229.3 1.3 dynamic-slice
  230.8 22.8 %all-reduce.1 = f32[16,8,8]{0,2,1:T(8,128)S(1)} all-reduce(f32[16,8,8]{0,2,1:T(8,128)S(1)} %copy.58), channel_id=5, replica_groups=mesh['node'=16,'local'=8,'edata'=4] {'local'}, use_global_device_ids=true, to_apply=%region_11.12.clone | all-reduce | flops 1024 | bytes 8192
  253.6 0.7 constant_dynamic-slice_fusion
  254.2 0.7 copy.59
  254.9 12.7 %all-to-all-start.4 = ((f32[16,1,8]{2,1,0:T(1,128)}), f32[16,1,8]{2,1,0:T(1,128)S(1)}, u32[]{:S(2)}, u32[]{:S(2)}) async-start(f32[16,1,8]{2,1,0:T(1,128)} %copy.59), calls=%async_computation.4 | async-start | bytes 16384 | tf_op jit(solution)/shard_map/all_to_all | solution.py:87
  267.6 48.1 %all-reduce.6.cloned.1.call-done = f32[16,8,8,1024]{3,2,1,0:T(8,128)} async-done(((f32[16,8,8,1024]{3,2,1,0:T(8,128)}), f32[16,8,8,1024]{3,2,1,0:T(8,128)}) %all-reduce.6.cloned.1.call-update) | async-done | bytes 4194320
  315.7 2.5 constant_dynamic-slice_fusion.1
  318.2 14.4 %all-to-all-start.3 = ((f32[16,1,8,1024]{3,2,1,0:T(8,128)}), f32[16,1,8,1024]{3,2,1,0:T(8,128)S(1)}, u32[]{:S(2)}, u32[]{:S(2)}) async-start(f32[16,1,8,1024]{3,2,1,0:T(8,128)} %constant_dynamic-slice_fusion.1), calls=%async_computation.3 | async-start | bytes 1048576 | tf_op jit(solution)/shard_map/all_to_all | solution.py:86
  333.0 3.5 fusion.27
  336.5 1.8 fusion.9
  338.4 0.7 fusion.23
  339.1 9.9 %select_select_fusion = f32[512]{0:T(512)S(1)} fusion(s32[512]{0:T(512)S(1)} %bitcast.79, f32[]{:T(128)} %bitcast.13, f32[]{:T(128)} %bitcast.14, f32[]{:T(128)} %bitcast.15, f32[]{:T(128)} %bitcast.16, f32[]{:T(128)} %bitcast.17, f32[]{:T(128)} %bitcast.18, f32[]{:T(128)} %bitcast.19, f32[]{:T(128)} %bitcast.20, f32[]{:T(128)} %bitcast.21, f32[]{:T(128)} %bitcast.22, ...), kind=kLoop, calls=%fused_computation.42 | loop fusion | flops 15360 | bytes 4160 | tf_op jit(solution)/shard_map/gather | solution.py:100
  349.3 0.7 copy.62
  349.9 12.0 %all-to-all-done.3 = f32[16,1,8,1024]{3,2,1,0:T(8,128)S(1)} async-done(((f32[16,1,8,1024]{3,2,1,0:T(8,128)}), f32[16,1,8,1024]{3,2,1,0:T(8,128)S(1)}, u32[]{:S(2)}, u32[]{:S(2)}) %all-to-all-start.3) | async-done | bytes 524320 | tf_op jit(solution)/shard_map/all_to_all | solution.py:86
  362.0 1.9 gather_fusion
  363.9 2.3 reshape.164
  366.2 5.0 %select_reduce_fusion = bf16[256,1024]{1,0:T(8,128)(2,1)} fusion(f32[256,2,1024]{2,1,0:T(2,128)} %reshape.164, pred[256,2]{1,0:T(8,128)(4,1)S(1)} %get-tuple-element.23), kind=kLoop, calls=%fused_computation.1 | loop fusion | flops 786432 | bytes 2621952 | tf_op jit(solution)/shard_map/reduce_sum | solution.py:96
  (57 shorter events, 3.4 us)
Async XLA Ops:
  7.2 69.4 %copy-start = (bf16[1024,256]{1,0:T(8,128)(2,1)S(1)}, bf16[1024,256]{1,0:T(8,128)(2,1)}, u32[]{:S(2)}) copy-start(bf16[1024,256]{1,0:T(8,128)(2,1)} %param.10) | copy-start | bytes 1572868
  7.2 42.0 %copy-start.2 = (bf16[256,1024]{1,0:T(8,128)(2,1)S(1)}, bf16[256,1024]{1,0:T(8,128)(2,1)}, u32[]{:S(2)}) copy-start(bf16[256,1024]{1,0:T(8,128)(2,1)} %param.7) | copy-start | bytes 1572868
  7.2 69.4 %all-gather.7.cloned.1.call-start = ((), (), s32[]{:S(2)}) async-start(), calls=%async_computation.6 | async-start | bytes 2359296 | tf_op jit(solution)/shard_map/all_gather | solution.py:53
  49.1 62.8 %all-gather.5.cloned.1.call-start = ((), (), s32[]{:S(2)}) async-start(), calls=%async_computation.5 | async-start | bytes 2359296 | tf_op jit(solution)/shard_map/all_gather | solution.py:54
  71.3 152.7 %all-reduce.8.cloned.1.call-start = ((), (), s32[]{:S(2)}) async-start(), calls=%async_computation.8 | async-start | bytes 4194304 | tf_op jit(solution)/shard_map/psum | solution.py:65
  76.6 35.4 %copy-start.5 = (bf16[256,1024]{1,0:T(8,128)(2,1)S(1)}, bf16[256,1024]{1,0:T(8,128)(2,1)}, u32[]{:S(2)}) copy-start(bf16[256,1024]{1,0:T(8,128)(2,1)} %param.11) | copy-start | bytes 1572868
  115.3 0.7 copy-start.3
  115.3 200.4 %all-reduce.6.cloned.1.call-start = ((), (), s32[]{:S(2)}) async-start(), calls=%async_computation.7 | async-start | bytes 8388608
  254.9 63.3 %all-to-all-start.4 = ((f32[16,1,8]{2,1,0:T(1,128)}), f32[16,1,8]{2,1,0:T(1,128)S(1)}, u32[]{:S(2)}, u32[]{:S(2)}) async-start(f32[16,1,8]{2,1,0:T(1,128)} %copy.59), calls=%async_computation.4 | async-start | bytes 16384 | tf_op jit(solution)/shard_map/all_to_all | solution.py:87
  318.2 43.7 %all-to-all-start.3 = ((f32[16,1,8,1024]{3,2,1,0:T(8,128)}), f32[16,1,8,1024]{3,2,1,0:T(8,128)S(1)}, u32[]{:S(2)}, u32[]{:S(2)}) async-start(f32[16,1,8,1024]{3,2,1,0:T(8,128)} %constant_dynamic-slice_fusion.1), calls=%async_computation.3 | async-start | bytes 1048576 | tf_op jit(solution)/shard_map/all_to_all | solution.py:86
  333.0 3.5 copy-start.1
  333.0 3.5 copy-start.4
Sparse Core Ops, SparseCore 0:
  49.2 27.2 all-gather.6
  78.7 33.2 all-gather.4
  115.5 108.4 all-reduce.7
  229.5 86.2 all-reduce.5
where the time goes:
time: 382 us; the launch traced here: 378 us
  waiting for transfers between devices  164 us (43%)
  blocking collectives  123 us (32%)
  starting transfers between devices  27.3 us (7%)
  other arithmetic  18.7 us (5%)
  matrix products  16.1 us (4%)
  local copies, waits for them, and re-layouts  14.7 us (4%)
  between operations  14 us (4%)
    psum x1, waiting for transfers between devices, body(): pre_act, back_grad = lax.psum((pre_part, back_part), 'edata')  66.3 us
    unnamed x5, waiting for transfers between devices  48.1 us
    all_to_all x1, blocking collectives, body(): lax.all_to_all(spread_x, 'node', split_axis=0, concat_axis=0, tiled=True)  38 us
    all_gather x1, waiting for transfers between devices, body(): lax.all_gather(got_dy[:, None], 'local', axis=1, tiled=True)  32 us
    all_to_all x1, blocking collectives, body(): lax.all_to_all(spread_gate, 'node', split_axis=0, concat_axis=0, tiled=True)  27.8 us
    unnamed x1, blocking collectives  22.8 us
    all_to_all x1, blocking collectives, body(): lax.all_to_all(spread_dy, 'node', split_axis=0, concat_axis=0, tiled=True)  21.9 us
    all_to_all x1, starting transfers between devices, body(): lax.all_to_all(reduced_x, 'node', split_axis=0, concat_axis=0, tiled=True)  14.4 us
  transfers between devices with their start and end apart: 6, of which 5 were waited for; matrix products, arithmetic and copies ran while one was open for 7% of the time, Pallas kernels for 0%

commit v1 on v0

v1 whole, which is shorter than its diff:
```python
import functools

import jax
import jax.numpy as jnp
from jax import lax
from jax.experimental import pallas as pl
from jax.experimental.pallas import tpu as pltpu
from jax.sharding import PartitionSpec as P

MESH = pl.DeviceIdType.MESH
BF, F32 = jnp.bfloat16, jnp.float32
WINDOW = 2
CAP = 8
LANES = 128
X_CHIPS, ZH_CHIPS = 4, 4


def gelu_pair(pre):
    coefficient = 0.7978845608028654
    tanh_val = jnp.tanh(coefficient * (pre + 0.044715 * pre * pre * pre))
    activation = 0.5 * pre * (1.0 + tanh_val)
    slopes = 0.5 * (1.0 + tanh_val) + 0.5 * pre * (1.0 - tanh_val * tanh_val) * coefficient * (
        1.0 + 3.0 * 0.044715 * pre * pre
    )
    return activation, slopes


def split(value):
    high = value.astype(BF)
    return high, (value - high.astype(F32)).astype(BF)


def dot_nt(a, b):
    return lax.dot_general(a, b, (((1,), (1,)), ((), ())), preferred_element_type=F32)


def dot_tn(a, b):
    return lax.dot_general(a, b, (((0,), (0,)), ((), ())), preferred_element_type=F32)


def wait_for(ref, sem):
    pltpu.make_async_copy(ref, ref, sem).wait()


def kernel(
    dims,
    tokens, grad_out, routes, gates, w_in, w_out,
    o_tokens, o_gates, o_w_in, o_w_out,
    zbuf, rows, xa, dya, part, rs_out, rs_in, res, res_sib, w_sib, dpa, sca, cs, cr, zs, zr, own,
    z_s, z_r, xy_s, xy_r, sib_s, sib_r, rs_s, rs_r, ag_s, ag_r, ds_s, ds_r, c_s, c_r, zc_s, zc_r, w_s, w_r,
):
    nx, nzh, ny, nzl = dims
    units = nx * ny
    half = units // 2
    hr = half * CAP
    n_half = 2 * nzh
    tok, fe = tokens.shape
    hid = w_in.shape[1]
    fh = fe // 2
    lat = 2 * (nzl - 1)
    offsets = [0] + [o for o in range(1, nzh) if o != nzh // 2] + ([nzh // 2] if nzh > 1 else [])

    node, local, zl = lax.axis_index("node"), lax.axis_index("local"), lax.axis_index("edata")
    x, zh, y, c = node // nzh, node % nzh, local // 2, local % 2
    me = y * nx + x
    sibling = (node, y * 2 + 1 - c, zl)

    def at_unit(u):
        return ((u % nx) * nzh + zh, (u // nx) * 2 + c, zl)

    def at_zh(other):
        return (x * nzh + other, local, zl)

    def offset_of(i):
        if nzh == 4:
            return jnp.where(i == 2, 3, jnp.where(i == 3, 2, i))
        return i

    pos = (nzl - 1 - zl, zl)
    ahead = (zl - 1, zl + 1)
    behind = (zl + 1, zl - 1)

    def remote(src, dst, send_sem, recv_sem, device):
        return pltpu.make_async_remote_copy(
            src_ref=src, dst_ref=dst, send_sem=send_sem, recv_sem=recv_sem, device_id=device, device_id_type=MESH
        )

    barrier = pltpu.get_barrier_semaphore()

    def greet(device):
        pl.semaphore_signal(barrier, inc=1, device_id=device, device_id_type=MESH)

    greet(sibling)
    for o in range(1, nzh):
        greet(at_zh((zh + o) % nzh))

    @pl.loop(1, units)
    def _(d):
        greet(at_unit((me + d) % units))

    @pl.when(zl > 0)
    def _():
        greet((node, local, zl - 1))

    @pl.when(zl < nzl - 1)
    def _():
        greet((node, local, zl + 1))

    lane = lax.broadcasted_iota(jnp.int32, (tok, LANES), 1)
    expert_of, place_of = (lane // CAP) % WINDOW, lane % CAP
    r0, r1 = routes[:, 0:1], routes[:, 1:2]
    g0, g1 = gates[:, 0:1].astype(F32), gates[:, 1:2].astype(F32)
    named = (r0 == expert_of) | (r1 == expert_of)
    earlier = lax.broadcasted_iota(jnp.int32, (tok, tok), 1) < lax.broadcasted_iota(jnp.int32, (tok, tok), 0)
    position = jnp.dot(
        jnp.where(earlier, 1.0, 0.0).astype(BF), jnp.where(named, 1.0, 0.0).astype(BF), preferred_element_type=F32
    )
    taken = named & (position == place_of.astype(F32)) & (lane < 3 * WINDOW * CAP)
    hot = jnp.where(taken, 1.0, 0.0).astype(BF)
    send_x, send_dy = dot_tn(hot, tokens[...]), dot_tn(hot, grad_out[...])
    for e in range(WINDOW):
        gate_e = jnp.where(r0 == e, g0, 0.0) + jnp.where(r1 == e, g1, 0.0)
        send_g = dot_tn(hot, jnp.broadcast_to(gate_e, (tok, LANES)).astype(BF))
        mine = slice(e * CAP, (e + 1) * CAP)
        zbuf[0, e, :, :fe] = jnp.concatenate([send_x[mine], send_dy[mine]], axis=0).astype(BF)
        zbuf[0, e, :, fe:] = jnp.concatenate([send_g[mine], send_g[mine]], axis=0).astype(BF)

    greeted = 1 + (nzh - 1) + (units - 1) + jnp.where(zl > 0, 1, 0) + jnp.where(zl < nzl - 1, 1, 0)
    pl.semaphore_wait(barrier, greeted)

    def dispatch(i):
        @pl.loop(0, units)
        def _(d):
            u = (me + d) % units
            src = zbuf.at[i, (u % nx) // (nx // 2)]
            dst = rows.at[i, c, me]

            @pl.when(d > 0)
            def _():
                remote(src, dst, xy_s.at[i], xy_r.at[i], at_unit(u)).start()

            @pl.when(d == 0)
            def _():
                pltpu.make_async_copy(src, dst, xy_r.at[i]).start()

    dispatch(0)
    for i in range(1, nzh):
        remote(zbuf.at[0], zbuf.at[i], z_s.at[i], z_r.at[i], at_zh((zh + nzh - offsets[i]) % nzh)).start()
    remote(w_in, w_sib, w_s, w_r, sibling).start()

    def pass_on(h, t, pre, back):
        high, low = split(pre)
        rs_out[h, t, :, 0:hid] = high
        rs_out[h, t, :, hid : 2 * hid] = low
        rs_out[h, t, :, 2 * hid :] = back.astype(BF)
        remote(
            rs_out.at[h, t], rs_in.at[h, t], rs_s.at[h], rs_r.at[h, t], (node, local, ahead[h])
        ).start()

    def send_back(h, t):
        remote(
            res.at[h, t], res.at[h, t], ag_s.at[h], ag_r.at[h, t], (node, local, behind[h])
        ).start()

    def partial_products(t):
        i, j = t // 2, t % 2
        parity = (c + j) % 2

        @pl.when(j == 0)
        def _():
            wait_for(rows.at[i, c], xy_r.at[i])
            remote(rows.at[i, c], rows.at[i, c], sib_s.at[i], sib_r.at[i], sibling).start()

        @pl.when(j == 1)
        def _():
            wait_for(rows.at[i, 1 - c], sib_r.at[i])

        for q in range(half):
            a = rows[i, parity, 2 * q, :, :fe].astype(F32)
            b = rows[i, parity, 2 * q + 1, :, :fe].astype(F32)
            xa[t, q * 16 : (q + 1) * 16, :] = jnp.concatenate([a[:CAP], b[:CAP]], axis=0).astype(BF)
            dya[t, q * 16 : (q + 1) * 16, :] = jnp.concatenate([a[CAP:], b[CAP:]], axis=0).astype(BF)
        part[t, :, :hid] = jnp.dot(xa[t], w_in[...], preferred_element_type=F32)
        part[t, :, hid:] = dot_nt(dya[t], w_out[...])
        for h in range(2):

            @pl.when(pos[h] == 0)
            def _():
                mine = slice(h * hr, (h + 1) * hr)
                pass_on(h, t, part[t, mine, :hid], part[t, mine, hid:])

    def sum_step(h, t):
        wait_for(rs_in.at[h, t], rs_r.at[h, t])
        mine = slice(h * hr, (h + 1) * hr)
        came = rs_in[h, t].astype(F32)
        pre = (came[:, :hid] + came[:, hid : 2 * hid]) + part[t, mine, :hid]
        back = came[:, 2 * hid :] + part[t, mine, hid:]

        @pl.when(pos[h] < nzl - 1)
        def _():
            pass_on(h, t, pre, back)

        @pl.when(pos[h] == nzl - 1)
        def _():
            i, parity = t // 2, (c + t % 2) % 2
            gate = rows[i, parity, h * half : (h + 1) * half, :, fe:].astype(F32)[:, :CAP]
            gate = gate.reshape(hr, LANES)
            gate = jnp.concatenate([gate] * (hid // LANES), axis=1)
            activation, slopes = gelu_pair(pre)
            res[h, t, :hr, :] = (gate * back * slopes).astype(BF)
            res[h, t, hr : 2 * hr, :] = (gate * activation).astype(BF)
            sums = jnp.sum(activation * back, axis=1, keepdims=True)
            small_lane = lax.broadcasted_iota(jnp.int32, (CAP, LANES), 1)
            packed = jnp.zeros((CAP, LANES), F32)
            for u in range(half):
                packed = jnp.where(small_lane == h * half + u, sums[u * CAP : (u + 1) * CAP], packed)
            high = packed.astype(BF).astype(F32)
            both = jnp.concatenate([high, packed - high], axis=0)
            both = jnp.concatenate([both] * (hid // LANES), axis=1)
            res[h, t, 2 * hr :, :] = both.astype(BF)
            send_back(h, t)

    def back_step(h, t):
        wait_for(res.at[h, t], ag_r.at[h, t])

        @pl.when(pos[h] > 0)
        def _():
            send_back(h, t)

    def keep(t):
        for h in range(2):
            mine = pl.ds(pl.multiple_of(t * 2 * hr + h * hr, hr), hr)
            dpa[mine, :] = res[h, t, :hr, :]
            sca[mine, :] = res[h, t, hr : 2 * hr, :]

    def to_sibling(i):
        for h in range(2):
            remote(res.at[h, 2 * i + 1], res_sib.at[i, h], ds_s.at[i, h], ds_r.at[i, h], sibling).start()

    def combine(i):
        t = 2 * i
        for h in range(2):
            wait_for(res_sib.at[i, h], ds_r.at[i, h])

        @pl.when(i == 0)
        def _():
            wait_for(w_sib, w_r)

        d_own = jnp.concatenate([res[0, t, :hr, :], res[1, t, :hr, :]], axis=0)
        d_sib = jnp.concatenate([res_sib[i, 0, :hr, :], res_sib[i, 1, :hr, :]], axis=0)
        total = dot_nt(d_own, w_in[...]) + dot_nt(d_sib, w_sib[...])
        packed = jnp.zeros((CAP, LANES), F32)
        for h in range(2):
            for ref in (res[h, t, 2 * hr :, :LANES], res_sib[i, h, 2 * hr :, :LANES]):
                both = ref.astype(F32)
                packed = packed + (both[:CAP] + both[CAP:])
        small_lane = lax.broadcasted_iota(jnp.int32, (CAP, LANES), 1)
        for u in range(units):
            mine = total[u * CAP : (u + 1) * CAP]
            cs[i, u, :, :fh] = jnp.concatenate([mine[:, :fh], mine[:, fh:]], axis=0).astype(BF)
            gate = jnp.sum(jnp.where(small_lane == u, packed, 0.0), axis=1, keepdims=True)
            gate = jnp.broadcast_to(gate, (CAP, LANES))
            high = gate.astype(BF).astype(F32)
            cs[i, u, :, fh:] = jnp.concatenate([high, gate - high], axis=0).astype(BF)

        @pl.loop(0, units)
        def _(d):
            u = (me + d) % units

            @pl.when(d > 0)
            def _():
                remote(cs.at[i, u], cr.at[i, me], c_s.at[i], c_r.at[i], at_unit(u)).start()

            @pl.when(d == 0)
            def _():
                pltpu.make_async_copy(cs.at[i, u], cr.at[i, me], c_r.at[i]).start()

    def sum_units(i):
        wait_for(cr.at[i], c_r.at[i])
        for e in range(WINDOW):
            total = jnp.zeros((2 * CAP, fh + LANES), F32)
            for yy in range(ny):
                for xx in range(e * (nx // 2), (e + 1) * (nx // 2)):
                    total = total + cr[i, yy * nx + xx].astype(F32)

            @pl.when(i == 0)
            def _():
                own[e] = total

            @pl.when(i > 0)
            def _():
                gate = total[:CAP, fh:] + total[CAP:, fh:]
                high = gate.astype(BF).astype(F32)
                zs[i, e, :, :fh] = total[:, :fh].astype(BF)
                zs[i, e, :, fh:] = jnp.concatenate([high, gate - high], axis=0).astype(BF)

        @pl.when(i > 0)
        def _():
            remote(
                zs.at[i], zr.at[i], zc_s.at[i], zc_r.at[i], at_zh((zh + offset_of(i)) % nzh)
            ).start()

    slots = 2 * (nzh - 1) + 2 + lat + 1

    @pl.loop(0, slots)
    def _(s):
        for h in range(2):
            t = s - lat + pos[h]

            @pl.when((pos[h] < nzl - 1) & (t >= 0) & (t < n_half))
            def _():
                back_step(h, t)

        for h in range(2):
            t = s - pos[h]

            @pl.when((pos[h] > 0) & (t >= 0) & (t < n_half))
            def _():
                sum_step(h, t)

        @pl.when(s < n_half)
        def _():
            partial_products(s)

        @pl.when((s % 2 == 0) & (s // 2 + 1 < nzh))
        def _():
            i = s // 2 + 1
            wait_for(zbuf.at[i], z_r.at[i])
            dispatch(i)

        done = s - lat

        @pl.when((done >= 0) & (done < n_half))
        def _():
            keep(done)

            @pl.when(done % 2 == 1)
            def _():
                to_sibling(done // 2)

        @pl.when((done >= 2) & (done % 2 == 0))
        def _():
            combine(done // 2 - 1)

        @pl.when((done >= 4) & (done % 2 == 0))
        def _():
            sum_units(done // 2 - 2)

    tile = min(256, fe)

    @pl.loop(0, fe // tile)
    def _(m):
        cols = pl.ds(pl.multiple_of(m * tile, tile), tile)
        o_w_out[:, cols] = dot_tn(sca[...], dya[:, :, cols].reshape(n_half * 2 * hr, tile))

    sum_units(nzh - 1)

    @pl.loop(0, fe // tile)
    def _(m):
        cols = pl.ds(pl.multiple_of(m * tile, tile), tile)
        o_w_in[cols, :] = dot_tn(xa[:, :, cols].reshape(n_half * 2 * hr, tile), dpa[...])

    slot, gate_slot = [], []
    for i in range(1, nzh):
        wait_for(zr.at[i], zc_r.at[i])
    for e in range(WINDOW):
        total = own[e]
        for i in range(1, nzh):
            total = total + zr[i, e].astype(F32)
        slot.append(jnp.concatenate([total[:CAP, :fh], total[CAP:, :fh]], axis=1))
        gate_slot.append(total[:CAP, fh:] + total[CAP:, fh:])
    slot = jnp.concatenate(slot, axis=0)
    lane_half = lax.broadcasted_iota(jnp.int32, (CAP, LANES), 1) // (LANES // 2)
    gate_slot = jnp.concatenate([jnp.where(lane_half == e, gate_slot[e], 0.0) for e in range(WINDOW)], axis=0)

    def three(value):
        high = value.astype(BF).astype(F32)
        middle = (value - high).astype(BF).astype(F32)
        low = value - high - middle
        rest = jnp.zeros((LANES - 3 * WINDOW * CAP, value.shape[1]), F32)
        return jnp.concatenate([high, middle, low, rest], axis=0).astype(BF)

    o_tokens[...] = jnp.dot(hot, three(slot), preferred_element_type=F32).astype(BF)
    gate_rows = jnp.dot(hot, three(gate_slot), preferred_element_type=F32)
    first, second = gate_rows[:, 0:1], gate_rows[:, LANES // 2 : LANES // 2 + 1]
    for k, r in enumerate((r0, r1)):
        o_gates[:, k : k + 1] = jnp.where(r == 0, first, jnp.where(r == 1, second, 0.0))

    for i in range(1, nzh):
        wait_for(zbuf.at[0], z_s.at[i])
        wait_for(zs.at[i], zc_s.at[i])
    for i in range(nzh):
        wait_for(rows.at[i, 0, pl.ds(0, units - 1)], xy_s.at[i])
        wait_for(rows.at[i, 0], sib_s.at[i])
        wait_for(cs.at[i, pl.ds(0, units - 1)], c_s.at[i])
        for h in range(2):
            wait_for(res_sib.at[i, h], ds_s.at[i, h])
    wait_for(w_sib, w_s)
    for h in range(2):

        @pl.when(pos[h] < nzl - 1)
        def _():
            wait_for(rs_out.at[h], rs_s.at[h])

        @pl.when(pos[h] > 0)
        def _():
            wait_for(res.at[h], ag_s.at[h])


def body(dims, tokens, grad_out, routes, gates, w_in, w_out):
    nx, nzh, ny, nzl = dims
    units = nx * ny
    hr = units * CAP // 2
    n_half = 2 * nzh
    tok, fe = tokens.shape
    hid = w_in.shape[1]
    all_rows = n_half * 2 * hr
    vmem = pl.BlockSpec(memory_space=pltpu.VMEM)
    dma = pltpu.SemaphoreType.DMA
    return pl.pallas_call(
        functools.partial(kernel, dims),
        out_shape=(
            jax.ShapeDtypeStruct((tok, fe), BF),
            jax.ShapeDtypeStruct((tok, 2), F32),
            jax.ShapeDtypeStruct((fe, hid), F32),
            jax.ShapeDtypeStruct((hid, fe), F32),
        ),
        in_specs=[vmem] * 6,
        out_specs=(vmem,) * 4,
        scratch_shapes=[
            pltpu.VMEM((nzh, WINDOW, 2 * CAP, fe + LANES), BF),
            pltpu.VMEM((nzh, 2, units, 2 * CAP, fe + LANES), BF),
            pltpu.VMEM((n_half, 2 * hr, fe), BF),
            pltpu.VMEM((n_half, 2 * hr, fe), BF),
            pltpu.VMEM((n_half, 2 * hr, 2 * hid), F32),
            pltpu.VMEM((2, n_half, hr, 3 * hid), BF),
            pltpu.VMEM((2, n_half, hr, 3 * hid), BF),
            pltpu.VMEM((2, n_half, 2 * hr + 16, hid), BF),
            pltpu.VMEM((nzh, 2, 2 * hr + 16, hid), BF),
            pltpu.VMEM((fe, hid), BF),
            pltpu.VMEM((all_rows, hid), BF),
            pltpu.VMEM((all_rows, hid), BF),
            pltpu.VMEM((nzh, units, 2 * CAP, fe // 2 + LANES), BF),
            pltpu.VMEM((nzh, units, 2 * CAP, fe // 2 + LANES), BF),
            pltpu.VMEM((nzh, WINDOW, 2 * CAP, fe // 2 + LANES), BF),
            pltpu.VMEM((nzh, WINDOW, 2 * CAP, fe // 2 + LANES), BF),
            pltpu.VMEM((WINDOW, 2 * CAP, fe // 2 + LANES), F32),
            dma((nzh,)), dma((nzh,)),
            dma((nzh,)), dma((nzh,)),
            dma((nzh,)), dma((nzh,)),
            dma((2,)), dma((2, n_half)),
            dma((2,)), dma((2, n_half)),
            dma((nzh, 2)), dma((nzh, 2)),
            dma((nzh,)), dma((nzh,)),
            dma((nzh,)), dma((nzh,)),
            dma, dma,
        ],
        compiler_params=pltpu.CompilerParams(
            collective_id=0, has_side_effects=True, vmem_limit_bytes=56 * 1024 * 1024
        ),
    )(tokens, grad_out, routes, gates, w_in, w_out)


def solution(mesh):
    dims = (X_CHIPS, ZH_CHIPS, mesh.shape["local"] // 2, mesh.shape["edata"])
    in_specs = (
        P(("node", "local"), "edata"),
        P(("node", "local"), "edata"),
        P(("node", "local"), None),
        P(("node", "local"), None),
        P("edata", ("node", "local")),
        P(("node", "local"), "edata"),
    )
    out_specs = (
        P(("node", "local"), "edata"),
        P(("node", "local"), None),
        P("edata", ("node", "local")),
        P(("node", "local"), "edata"),
    )
    return jax.shard_map(
        functools.partial(body, dims), mesh=mesh, in_specs=in_specs, out_specs=out_specs, check_vma=False
    )
```

time: 382 us -> 111 us (0.29); the launches traced: 378 us -> 111 us
  waiting for transfers between devices: 164 us -> 0 us
  blocking collectives: 123 us -> 0 us
  Pallas kernels: 0 us -> 102 us
  starting transfers between devices: 27.3 us -> 0 us
  other arithmetic: 18.7 us -> 0 us
  matrix products: 16.1 us -> 0 us
  between operations: 14 us -> 0.66 us
  local copies, waits for them, and re-layouts: 14.7 us -> 8.33 us
    pallas_call x0 -> x1, Pallas kernels: none -> 102 us  [body(): pl.pallas_call(functools.partial(kernel, dims), out_shape=(jax.ShapeDtype...]
    all_to_all x3 -> x0, blocking collectives: 87.6 us -> none  [the longest x1 38 us: body(): lax.all_to_all(spread_x, 'node', split_axis=0, concat_axis=0, tiled=True)]
    psum x1 -> x0, waiting for transfers between devices: 66.3 us -> none  [body(): pre_act, back_grad = lax.psum((pre_part, back_part), 'edata')]
    unnamed x5 -> x0, waiting for transfers between devices: 48.1 us -> none
    all_gather x2 -> x0, waiting for transfers between devices: 37.3 us -> none  [the longest x1 32 us: body(): lax.all_gather(got_dy[:, None], 'local', axis=1, tiled=True)]
    all_to_all x2 -> x0, starting transfers between devices: 27.1 us -> none  [the longest x1 14.4 us: body(): lax.all_to_all(reduced_x, 'node', split_axis=0, concat_axis=0, tiled=True)]
    unnamed x1 -> x0, blocking collectives: 22.8 us -> none
    dot_general x7 -> x0, matrix products: 16.1 us -> none  [the longest x1 3.47 us: body(): lax.dot_general(x_rows, pre_grad, (((0,), (0,)), ((), ())), preferred_ele...]
  transfers between devices with their start and end apart: 6 -> 0, of which waited for: 5 -> 0; matrix products, arithmetic and copies ran while one was open for 7% -> 0% of each run, Pallas kernels for 0% -> 0%
where the time goes in v1:
time: 111 us
  Pallas kernels  102 us (92%)
  local copies, waits for them, and re-layouts  8.33 us (8%)
    pallas_call x1, Pallas kernels, body(): pl.pallas_call(functools.partial(kernel, dims), out_shape=(jax.ShapeDtype...  102 us
    unnamed x11, local copies, waits for them, and re-layouts  6.68 us

profile of v1, /device:TPU:1, one launch (start us, length us, event | category | flops | bytes accessed | tf_op | source)
XLA Modules:
  0.0 111.1 jit_solution(16656589865823416453)
XLA Ops:
  0.6 0.0 copy-start.2
  0.6 1.4 %copy.11.gates = bf16[256,2]{1,0:T(8,128)(2,1)} copy(bf16[256,2]{0,1:T(2,128)(2,1)} %param.9) | data formatting | bytes 2048 | tf_op args[3]
  2.1 0.0 copy-done.2
  2.1 0.8 copy.10.routes
  2.9 102.1 %shard_map.93 = (bf16[256,1024]{1,0:T(8,128)(2,1)}, f32[256,2]{1,0:T(8,128)}, f32[1024,256]{1,0:T(8,128)}, f32[256,1024]{1,0:T(8,128)}) custom-call(bf16[256,1024]{1,0:T(8,128)(2,1)} %tokens.1, bf16[256,1024]{1,0:T(8,128)(2,1)} %grad_out.1, s32[256,2]{1,0:T(8,128)} %copy.10.routes, bf16[256,2]{1,0:T(8,128)(2,1)} %copy.11.gates, bf16[1024,256]{1,0:T(8,128)(2,1)} %w_in.1, ...), custom_call_target="tpu_custom_call" | custom-call | tf_op jit(solution)/shard_map/pallas_call | solution.py:420
  105.0 0.0 copy-start.1
  105.0 1.6 %copy.12 = f32[256,2]{0,1:T(2,128)} copy(f32[256,2]{1,0:T(8,128)} %get-tuple-element.5) | data formatting | bytes 4096 | tf_op jit(solution)/shard_map/pallas_call | solution.py:420
  106.7 1.9 %copy.16 = bf16[256,1024]{1,0:T(8,128)(2,1)} copy(bf16[256,1024]{1,0:T(8,128)(2,1)} %get-tuple-element.12) | data formatting | bytes 1048576
  108.6 0.0 copy-done.1
  108.6 0.0 copy-start
  108.6 1.0 copy.17
  109.5 0.6 copy-done
  110.2 1.0 copy.18
Async XLA Ops:
  0.6 1.4 %copy-start.2 = (s32[256,2]{0,1:T(2,128)S(1)}, s32[256,2]{0,1:T(2,128)}, u32[]{:S(2)}) copy-start(s32[256,2]{0,1:T(2,128)} %param.8) | copy-start | bytes 6148
  105.0 3.5 %copy-start.1 = (f32[1024,256]{1,0:T(8,128)S(1)}, f32[1024,256]{1,0:T(8,128)}, u32[]{:S(2)}) copy-start(f32[1024,256]{1,0:T(8,128)} %get-tuple-element.14) | copy-start | bytes 3145732
  108.6 1.6 %copy-start = (f32[256,1024]{1,0:T(8,128)S(1)}, f32[256,1024]{1,0:T(8,128)}, u32[]{:S(2)}) copy-start(f32[256,1024]{1,0:T(8,128)} %get-tuple-element.15) | copy-start | bytes 3145732

commit v2 on v1

--- a/solution.py
+++ b/solution.py
@@ -13,6 +13,21 @@
 CAP = 8
 LANES = 128
 X_CHIPS, ZH_CHIPS = 4, 4
+HOP = 2
+OWN_LAST = False
+
+
+def half_chunks(nzh):
+    if OWN_LAST:
+        return [(0, 0)] + [(i, j) for i in range(1, nzh) for j in range(2)] + [(0, 1)]
+    return [(i, j) for i in range(nzh) for j in range(2)]
+
+
+def pick(table, t):
+    value = table[0]
+    for k in range(1, len(table)):
+        value = jnp.where(t == k, table[k], value)
+    return value
 
 
 def gelu_pair(pre):
@@ -44,10 +59,10 @@
 
 def kernel(
     dims,
-    tokens, grad_out, routes, gates, w_in, w_out,
+    tokens_hbm, grad_out_hbm, routes, gates, w_in_hbm, w_out_hbm,
     o_tokens, o_gates, o_w_in, o_w_out,
-    zbuf, rows, xa, dya, part, rs_out, rs_in, res, res_sib, w_sib, dpa, sca, cs, cr, zs, zr, own,
-    z_s, z_r, xy_s, xy_r, sib_s, sib_r, rs_s, rs_r, ag_s, ag_r, ds_s, ds_r, c_s, c_r, zc_s, zc_r, w_s, w_r,
+    tokens, grad_out, w_in, w_out, zbuf, rows, xa, dya, part, rs_out, rs_in, res, res_sib, w_sib, dpa, sca, cs, cr, zs, zr, own,
+    z_s, z_r, xy_s, xy_r, sib_s, sib_r, rs_s, rs_r, ag_s, ag_r, ds_s, ds_r, c_s, c_r, zc_s, zc_r, w_s, w_r, in_sem,
 ):
     nx, nzh, ny, nzl = dims
     units = nx * ny
@@ -57,8 +72,10 @@
     tok, fe = tokens.shape
     hid = w_in.shape[1]
     fh = fe // 2
-    lat = 2 * (nzl - 1)
-    offsets = [0] + [o for o in range(1, nzh) if o != nzh // 2] + ([nzh // 2] if nzh > 1 else [])
+    lat = 2 * HOP * (nzl - 1)
+    offsets = list(range(nzh))
+    near = [1, 3] if nzh == 4 else list(range(1, nzh))
+    far = 2 if nzh == 4 else None
 
     node, local, zl = lax.axis_index("node"), lax.axis_index("local"), lax.axis_index("edata")
     x, zh, y, c = node // nzh, node % nzh, local // 2, local % 2
@@ -71,10 +88,14 @@
     def at_zh(other):
         return (x * nzh + other, local, zl)
 
-    def offset_of(i):
-        if nzh == 4:
-            return jnp.where(i == 2, 3, jnp.where(i == 3, 2, i))
-        return i
+    order = half_chunks(nzh)
+    ends = {i: order.index((i, 1)) for i in range(nzh)}
+
+    def chunk_of(t):
+        return pick([i for i, _ in order], t)
+
+    def which_of(t):
+        return pick([j for _, j in order], t)
 
     pos = (nzl - 1 - zl, zl)
     ahead = (zl - 1, zl + 1)
@@ -85,6 +106,15 @@
             src_ref=src, dst_ref=dst, send_sem=send_sem, recv_sem=recv_sem, device_id=device, device_id_type=MESH
         )
 
+    loads = [
+        pltpu.make_async_copy(src, dst, in_sem.at[n])
+        for n, (src, dst) in enumerate(
+            ((tokens_hbm, tokens), (grad_out_hbm, grad_out), (w_in_hbm, w_in), (w_out_hbm, w_out))
+        )
+    ]
+    for load in loads:
+        load.start()
+
     barrier = pltpu.get_barrier_semaphore()
 
     def greet(device):
@@ -106,21 +136,25 @@
     def _():
         greet((node, local, zl + 1))
 
-    lane = lax.broadcasted_iota(jnp.int32, (tok, LANES), 1)
-    expert_of, place_of = (lane // CAP) % WINDOW, lane % CAP
-    r0, r1 = routes[:, 0:1], routes[:, 1:2]
-    g0, g1 = gates[:, 0:1].astype(F32), gates[:, 1:2].astype(F32)
+    slot_rows = 3 * WINDOW * CAP
+    row = lax.broadcasted_iota(jnp.int32, (slot_rows, tok), 0)
+    expert_of, place_of = (row // CAP) % WINDOW, row % CAP
+    r0, r1 = routes[0:1, :], routes[1:2, :]
+    g0, g1 = gates[0:1, :].astype(F32), gates[1:2, :].astype(F32)
     named = (r0 == expert_of) | (r1 == expert_of)
-    earlier = lax.broadcasted_iota(jnp.int32, (tok, tok), 1) < lax.broadcasted_iota(jnp.int32, (tok, tok), 0)
+    earlier = lax.broadcasted_iota(jnp.int32, (tok, tok), 0) < lax.broadcasted_iota(jnp.int32, (tok, tok), 1)
     position = jnp.dot(
-        jnp.where(earlier, 1.0, 0.0).astype(BF), jnp.where(named, 1.0, 0.0).astype(BF), preferred_element_type=F32
+        jnp.where(named, 1.0, 0.0).astype(BF), jnp.where(earlier, 1.0, 0.0).astype(BF), preferred_element_type=F32
     )
-    taken = named & (position == place_of.astype(F32)) & (lane < 3 * WINDOW * CAP)
-    hot = jnp.where(taken, 1.0, 0.0).astype(BF)
-    send_x, send_dy = dot_tn(hot, tokens[...]), dot_tn(hot, grad_out[...])
+    hot_f = jnp.where(named & (position == place_of.astype(F32)), 1.0, 0.0)
+    hot = hot_f.astype(BF)
+    send_g = jnp.sum(hot_f * jnp.where(r0 == expert_of, g0, g1), axis=1, keepdims=True)
+    send_g = jnp.broadcast_to(send_g, (slot_rows, LANES))
+    loads[0].wait()
+    send_x = jnp.dot(hot, tokens[...], preferred_element_type=F32)
+    loads[1].wait()
+    send_dy = jnp.dot(hot, grad_out[...], preferred_element_type=F32)
     for e in range(WINDOW):
-        gate_e = jnp.where(r0 == e, g0, 0.0) + jnp.where(r1 == e, g1, 0.0)
-        send_g = dot_tn(hot, jnp.broadcast_to(gate_e, (tok, LANES)).astype(BF))
         mine = slice(e * CAP, (e + 1) * CAP)
         zbuf[0, e, :, :fe] = jnp.concatenate([send_x[mine], send_dy[mine]], axis=0).astype(BF)
         zbuf[0, e, :, fe:] = jnp.concatenate([send_g[mine], send_g[mine]], axis=0).astype(BF)
@@ -143,10 +177,30 @@
             def _():
                 pltpu.make_async_copy(src, dst, xy_r.at[i]).start()
 
+    for i in near:
+        remote(zbuf.at[0], zbuf.at[i], z_s.at[i], z_r.at[i], at_zh((zh + nzh - offsets[i]) % nzh)).start()
     dispatch(0)
-    for i in range(1, nzh):
-        remote(zbuf.at[0], zbuf.at[i], z_s.at[i], z_r.at[i], at_zh((zh + nzh - offsets[i]) % nzh)).start()
+    loads[2].wait()
     remote(w_in, w_sib, w_s, w_r, sibling).start()
+    loads[3].wait()
+
+    def arrive(i):
+        if far is None:
+            wait_for(zbuf.at[i], z_r.at[i])
+        else:
+
+            @pl.when(i == 1)
+            def _():
+                for e, k in enumerate(near):
+                    wait_for(zbuf.at[k], z_r.at[k])
+                    remote(
+                        zbuf.at[k, e], zbuf.at[far, e], z_s.at[nzh + e], z_r.at[nzh + e], at_zh((zh + nzh - k) % nzh)
+                    ).start()
+
+            @pl.when(i == far)
+            def _():
+                for e in range(WINDOW):
+                    wait_for(zbuf.at[far, e], z_r.at[nzh + e])
 
     def pass_on(h, t, pre, back):
         high, low = split(pre)
@@ -163,7 +217,7 @@
         ).start()
 
     def partial_products(t):
-        i, j = t // 2, t % 2
+        i, j = chunk_of(t), which_of(t)
         parity = (c + j) % 2
 
         @pl.when(j == 0)
@@ -202,7 +256,7 @@
 
         @pl.when(pos[h] == nzl - 1)
         def _():
-            i, parity = t // 2, (c + t % 2) % 2
+            i, parity = chunk_of(t), (c + which_of(t)) % 2
             gate = rows[i, parity, h * half : (h + 1) * half, :, fe:].astype(F32)[:, :CAP]
             gate = gate.reshape(hr, LANES)
             gate = jnp.concatenate([gate] * (hid // LANES), axis=1)
@@ -235,16 +289,12 @@
 
     def to_sibling(i):
         for h in range(2):
-            remote(res.at[h, 2 * i + 1], res_sib.at[i, h], ds_s.at[i, h], ds_r.at[i, h], sibling).start()
+            remote(res.at[h, pick([ends[k] for k in range(nzh)], i)], res_sib.at[i, h], ds_s.at[i, h], ds_r.at[i, h], sibling).start()
 
     def combine(i):
-        t = 2 * i
+        t = pick([order.index((k, 0)) for k in range(nzh)], i)
         for h in range(2):
             wait_for(res_sib.at[i, h], ds_r.at[i, h])
-
-        @pl.when(i == 0)
-        def _():
-            wait_for(w_sib, w_r)
 
         d_own = jnp.concatenate([res[0, t, :hr, :], res[1, t, :hr, :]], axis=0)
         d_sib = jnp.concatenate([res_sib[i, 0, :hr, :], res_sib[i, 1, :hr, :]], axis=0)
@@ -297,65 +347,76 @@
         @pl.when(i > 0)
         def _():
             remote(
-                zs.at[i], zr.at[i], zc_s.at[i], zc_r.at[i], at_zh((zh + offset_of(i)) % nzh)
+                zs.at[i], zr.at[i], zc_s.at[i], zc_r.at[i], at_zh((zh + pick(offsets, i)) % nzh)
             ).start()
 
-    slots = 2 * (nzh - 1) + 2 + lat + 1
-
-    @pl.loop(0, slots)
+    tile = min(256, fe)
+
+    @pl.loop(0, n_half + lat)
     def _(s):
-        for h in range(2):
-            t = s - lat + pos[h]
+        @pl.when(s < n_half)
+        def _():
+            partial_products(s)
+
+        for h in range(2):
+            t = s - HOP * pos[h]
+
+            @pl.when((pos[h] > 0) & (t >= 0) & (t < n_half))
+            def _():
+                sum_step(h, t)
+
+        for h in range(2):
+            t = s - lat + HOP * pos[h]
 
             @pl.when((pos[h] < nzl - 1) & (t >= 0) & (t < n_half))
             def _():
                 back_step(h, t)
 
-        for h in range(2):
-            t = s - pos[h]
-
-            @pl.when((pos[h] > 0) & (t >= 0) & (t < n_half))
-            def _():
-                sum_step(h, t)
-
-        @pl.when(s < n_half)
-        def _():
-            partial_products(s)
-
-        @pl.when((s % 2 == 0) & (s // 2 + 1 < nzh))
-        def _():
-            i = s // 2 + 1
-            wait_for(zbuf.at[i], z_r.at[i])
+        @pl.when(s + 1 < nzh)
+        def _():
+            i = s + 1
+
+            arrive(i)
             dispatch(i)
 
         done = s - lat
 
-        @pl.when((done >= 0) & (done < n_half))
-        def _():
+        @pl.when(done >= 0)
+        def _():
+            @pl.when(done == 0)
+            def _():
+                wait_for(w_sib, w_r)
+
             keep(done)
 
-            @pl.when(done % 2 == 1)
-            def _():
-                to_sibling(done // 2)
-
-        @pl.when((done >= 2) & (done % 2 == 0))
-        def _():
-            combine(done // 2 - 1)
-
-        @pl.when((done >= 4) & (done % 2 == 0))
-        def _():
-            sum_units(done // 2 - 2)
-
-    tile = min(256, fe)
-
-    @pl.loop(0, fe // tile)
-    def _(m):
-        cols = pl.ds(pl.multiple_of(m * tile, tile), tile)
-        o_w_out[:, cols] = dot_tn(sca[...], dya[:, :, cols].reshape(n_half * 2 * hr, tile))
-
-    sum_units(nzh - 1)
-
-    @pl.loop(0, fe // tile)
+            @pl.when(which_of(done) == 1)
+            def _():
+                to_sibling(chunk_of(done))
+
+        @pl.when((done >= 1) & (which_of(done - 1) == 1))
+        def _():
+            combine(chunk_of(done - 1))
+
+        @pl.when((done >= 4) & (which_of(done - 4) == 1))
+        def _():
+            sum_units(chunk_of(done - 4))
+
+    def finish_w_out(first, last):
+        @pl.loop(first, last)
+        def _(m):
+            cols = pl.ds(pl.multiple_of(m * tile, tile), tile)
+            o_w_out[:, cols] = dot_tn(sca[...], dya[:, :, cols].reshape(n_half * 2 * hr, tile))
+
+    tiles = fe // tile
+    finish_w_out(0, tiles // 2)
+    combine(order[-1][0])
+    late = [i for t, (i, j) in enumerate(order) if j == 1 and t >= n_half - 4]
+    for i in late[:-1]:
+        sum_units(i)
+    finish_w_out(tiles // 2, tiles)
+    sum_units(late[-1])
+
+    @pl.loop(0, tiles)
     def _(m):
         cols = pl.ds(pl.multiple_of(m * tile, tile), tile)
         o_w_in[cols, :] = dot_tn(xa[:, :, cols].reshape(n_half * 2 * hr, tile), dpa[...])
@@ -370,25 +431,22 @@
         slot.append(jnp.concatenate([total[:CAP, :fh], total[CAP:, :fh]], axis=1))
         gate_slot.append(total[:CAP, fh:] + total[CAP:, fh:])
     slot = jnp.concatenate(slot, axis=0)
-    lane_half = lax.broadcasted_iota(jnp.int32, (CAP, LANES), 1) // (LANES // 2)
-    gate_slot = jnp.concatenate([jnp.where(lane_half == e, gate_slot[e], 0.0) for e in range(WINDOW)], axis=0)
-
-    def three(value):
-        high = value.astype(BF).astype(F32)
-        middle = (value - high).astype(BF).astype(F32)
-        low = value - high - middle
-        rest = jnp.zeros((LANES - 3 * WINDOW * CAP, value.shape[1]), F32)
-        return jnp.concatenate([high, middle, low, rest], axis=0).astype(BF)
-
-    o_tokens[...] = jnp.dot(hot, three(slot), preferred_element_type=F32).astype(BF)
-    gate_rows = jnp.dot(hot, three(gate_slot), preferred_element_type=F32)
-    first, second = gate_rows[:, 0:1], gate_rows[:, LANES // 2 : LANES // 2 + 1]
+    high = slot.astype(BF).astype(F32)
+    middle = (slot - high).astype(BF).astype(F32)
+    o_tokens[...] = dot_tn(hot, jnp.concatenate([high, middle, slot - high - middle], axis=0).astype(BF)).astype(BF)
+    gate_slot = jnp.concatenate(gate_slot, axis=0)
+    gate_slot = jnp.concatenate([gate_slot] * (tok // LANES), axis=1) * hot_f[: WINDOW * CAP]
     for k, r in enumerate((r0, r1)):
-        o_gates[:, k : k + 1] = jnp.where(r == 0, first, jnp.where(r == 1, second, 0.0))
+        kept = jnp.where(r == expert_of[: WINDOW * CAP], gate_slot, 0.0)
+        o_gates[k : k + 1, :] = jnp.sum(kept, axis=0, keepdims=True)
 
     for i in range(1, nzh):
+        wait_for(zs.at[i], zc_s.at[i])
+    for i in near:
         wait_for(zbuf.at[0], z_s.at[i])
-        wait_for(zs.at[i], zc_s.at[i])
+    if far is not None:
+        for e in range(WINDOW):
+            wait_for(zbuf.at[0, e], z_s.at[nzh + e])
     for i in range(nzh):
         wait_for(rows.at[i, 0, pl.ds(0, units - 1)], xy_s.at[i])
         wait_for(rows.at[i, 0], sib_s.at[i])
@@ -415,19 +473,23 @@
     tok, fe = tokens.shape
     hid = w_in.shape[1]
     all_rows = n_half * 2 * hr
-    vmem = pl.BlockSpec(memory_space=pltpu.VMEM)
+    vmem, hbm = pl.BlockSpec(memory_space=pltpu.VMEM), pl.BlockSpec(memory_space=pltpu.HBM)
     dma = pltpu.SemaphoreType.DMA
-    return pl.pallas_call(
+    grad_tokens, grad_gates, grad_w_in, grad_w_out = pl.pallas_call(
         functools.partial(kernel, dims),
         out_shape=(
-            jax.ShapeDtypeStruct((tok, fe), BF),
-            jax.ShapeDtypeStruct((tok, 2), F32),
-            jax.ShapeDtypeStruct((fe, hid), F32),
-            jax.ShapeDtypeStruct((hid, fe), F32),
+            pltpu.VMEM((tok, fe), BF),
+            pltpu.VMEM((2, tok), F32),
+            pltpu.VMEM((fe, hid), F32),
+            pltpu.VMEM((hid, fe), F32),
         ),
-        in_specs=[vmem] * 6,
+        in_specs=[hbm, hbm, vmem, vmem, hbm, hbm],
         out_specs=(vmem,) * 4,
         scratch_shapes=[
+            pltpu.VMEM((tok, fe), BF),
+            pltpu.VMEM((tok, fe), BF),
+            pltpu.VMEM((fe, hid), BF),
+            pltpu.VMEM((hid, fe), BF),
             pltpu.VMEM((nzh, WINDOW, 2 * CAP, fe + LANES), BF),
             pltpu.VMEM((nzh, 2, units, 2 * CAP, fe + LANES), BF),
             pltpu.VMEM((n_half, 2 * hr, fe), BF),
@@ -445,7 +507,7 @@
             pltpu.VMEM((nzh, WINDOW, 2 * CAP, fe // 2 + LANES), BF),
             pltpu.VMEM((nzh, WINDOW, 2 * CAP, fe // 2 + LANES), BF),
             pltpu.VMEM((WINDOW, 2 * CAP, fe // 2 + LANES), F32),
-            dma((nzh,)), dma((nzh,)),
+            dma((nzh + 2,)), dma((nzh + 2,)),
             dma((nzh,)), dma((nzh,)),
             dma((nzh,)), dma((nzh,)),
             dma((2,)), dma((2, n_half)),
@@ -454,11 +516,13 @@
             dma((nzh,)), dma((nzh,)),
             dma((nzh,)), dma((nzh,)),
             dma, dma,
+            dma((4,)),
         ],
         compiler_params=pltpu.CompilerParams(
-            collective_id=0, has_side_effects=True, vmem_limit_bytes=56 * 1024 * 1024
+            collective_id=0, has_side_effects=True, vmem_limit_bytes=58 * 1024 * 1024
         ),
-    )(tokens, grad_out, routes, gates, w_in, w_out)
+    )(tokens, grad_out, routes.T, gates.T, w_in, w_out)
+    return grad_tokens, grad_gates.T, grad_w_in, grad_w_out
 
 
 def solution(mesh):

time: 111 us -> 99.9 us (0.900)
  Pallas kernels: 102 us -> 95 us
  local copies, waits for them, and re-layouts: 8.33 us -> 3.31 us
    pallas_call x1, Pallas kernels: 102 us -> 95 us  [body(): pl.pallas_call(functools.partial(kernel, dims), out_shape=(pltpu.VMEM((to...]
    unnamed x11 -> x4, local copies, waits for them, and re-layouts: 6.68 us -> 3.31 us
    pallas_call x1 -> x0, local copies, waits for them, and re-layouts: 1.65 us -> none  [body(): pl.pallas_call(functools.partial(kernel, dims), out_shape=(jax.ShapeDtype...]
where the time goes in v2:
time: 99.9 us; the launch traced here: 99 us
  Pallas kernels  95 us (95%)
  local copies, waits for them, and re-layouts  3.31 us (3%)
    pallas_call x1, Pallas kernels, body(): pl.pallas_call(functools.partial(kernel, dims), out_shape=(pltpu.VMEM((to...  95 us
    unnamed x4, local copies, waits for them, and re-layouts  3.31 us

profile of v2, /device:TPU:1, one launch (start us, length us, event | category | flops | bytes accessed | tf_op | source)
XLA Modules:
  0.0 99.0 jit_solution(17847789783075839813)
XLA Ops:
  0.6 95.0 %shard_map.93 = (bf16[256,1024]{1,0:T(8,128)(2,1)S(1)}, f32[2,256]{1,0:T(2,128)S(1)}, f32[1024,256]{1,0:T(8,128)S(1)}, f32[256,1024]{1,0:T(8,128)S(1)}) custom-call(bf16[256,1024]{1,0:T(8,128)(2,1)} %tokens_hbm.1, bf16[256,1024]{1,0:T(8,128)(2,1)} %grad_out_hbm.1, s32[2,256]{1,0:T(2,128)} %bitcast.4, bf16[2,256]{1,0:T(2,128)(2,1)} %bitcast.5, ...), custom_call_target="tpu_custom_call" | custom-call | tf_op jit(solution)/shard_map/pallas_call | solution.py:478
  95.7 0.8 copy.14
  96.4 0.6 copy.15
  97.0 1.0 copy.16
  98.0 1.0 copy.17

commit v3 on v2

--- a/solution.py
+++ b/solution.py
@@ -162,45 +162,48 @@
     greeted = 1 + (nzh - 1) + (units - 1) + jnp.where(zl > 0, 1, 0) + jnp.where(zl < nzl - 1, 1, 0)
     pl.semaphore_wait(barrier, greeted)
 
-    def dispatch(i):
-        @pl.loop(0, units)
+    def dispatch(i, e):
+        @pl.loop(0, units // 2)
         def _(d):
-            u = (me + d) % units
-            src = zbuf.at[i, (u % nx) // (nx // 2)]
-            dst = rows.at[i, c, me]
-
-            @pl.when(d > 0)
-            def _():
-                remote(src, dst, xy_s.at[i], xy_r.at[i], at_unit(u)).start()
-
-            @pl.when(d == 0)
+            xx = e * (nx // 2) + (x + d) % (nx // 2)
+            yy = (y + d // (nx // 2)) % ny
+            src, dst = zbuf.at[i, e], rows.at[i, c, me]
+            itself = (d == 0) & (x // (nx // 2) == e)
+
+            @pl.when(jnp.logical_not(itself))
+            def _():
+                remote(src, dst, xy_s.at[i], xy_r.at[i], at_unit(yy * nx + xx)).start()
+
+            @pl.when(itself)
             def _():
                 pltpu.make_async_copy(src, dst, xy_r.at[i]).start()
 
     for i in near:
-        remote(zbuf.at[0], zbuf.at[i], z_s.at[i], z_r.at[i], at_zh((zh + nzh - offsets[i]) % nzh)).start()
-    dispatch(0)
+        for e in range(WINDOW):
+            remote(
+                zbuf.at[0, e], zbuf.at[i, e], z_s.at[i, e], z_r.at[i, e], at_zh((zh + nzh - offsets[i]) % nzh)
+            ).start()
+    for e in range(WINDOW):
+        dispatch(0, e)
     loads[2].wait()
     remote(w_in, w_sib, w_s, w_r, sibling).start()
     loads[3].wait()
 
-    def arrive(i):
-        if far is None:
-            wait_for(zbuf.at[i], z_r.at[i])
-        else:
-
-            @pl.when(i == 1)
-            def _():
-                for e, k in enumerate(near):
-                    wait_for(zbuf.at[k], z_r.at[k])
-                    remote(
-                        zbuf.at[k, e], zbuf.at[far, e], z_s.at[nzh + e], z_r.at[nzh + e], at_zh((zh + nzh - k) % nzh)
-                    ).start()
-
-            @pl.when(i == far)
-            def _():
-                for e in range(WINDOW):
-                    wait_for(zbuf.at[far, e], z_r.at[nzh + e])
+    def hand_on(i, e):
+        @pl.when(jnp.logical_not((i == near[-1]) & (e == len(near) - 1) & (far is not None)))
+        def _():
+            wait_for(zbuf.at[i, e], z_r.at[i, e])
+
+        dispatch(i, e)
+
+    def relay():
+        if far is not None:
+            for e, k in enumerate(near):
+                if k != 1:
+                    wait_for(zbuf.at[k, e], z_r.at[k, e])
+                remote(
+                    zbuf.at[k, e], zbuf.at[far, e], z_s.at[far, e], z_r.at[far, e], at_zh((zh + nzh - k) % nzh)
+                ).start()
 
     def pass_on(h, t, pre, back):
         high, low = split(pre)
@@ -304,16 +307,15 @@
             for ref in (res[h, t, 2 * hr :, :LANES], res_sib[i, h, 2 * hr :, :LANES]):
                 both = ref.astype(F32)
                 packed = packed + (both[:CAP] + both[CAP:])
-        small_lane = lax.broadcasted_iota(jnp.int32, (CAP, LANES), 1)
+        high = packed.astype(BF).astype(F32)
+        gates_of_all = jnp.concatenate([high, packed - high], axis=0).astype(BF)
         for u in range(units):
             mine = total[u * CAP : (u + 1) * CAP]
             cs[i, u, :, :fh] = jnp.concatenate([mine[:, :fh], mine[:, fh:]], axis=0).astype(BF)
-            gate = jnp.sum(jnp.where(small_lane == u, packed, 0.0), axis=1, keepdims=True)
-            gate = jnp.broadcast_to(gate, (CAP, LANES))
-            high = gate.astype(BF).astype(F32)
-            cs[i, u, :, fh:] = jnp.concatenate([high, gate - high], axis=0).astype(BF)
-
-        @pl.loop(0, units)
+            cs[i, u, :, fh:] = gates_of_all
+
+    def send_units(i, first, last):
+        @pl.loop(first, last)
         def _(d):
             u = (me + d) % units
 
@@ -354,6 +356,18 @@
 
     @pl.loop(0, n_half + lat)
     def _(s):
+        if nzh > 1:
+
+            @pl.when(s == 0)
+            def _():
+                hand_on(1, 0)
+                hand_on(1, 1)
+                relay()
+
+        @pl.when((s > 0) & (s < 2 * nzh - 3))
+        def _():
+            hand_on((s + 3) // 2, (s + 1) % 2)
+
         @pl.when(s < n_half)
         def _():
             partial_products(s)
@@ -372,13 +386,6 @@
             def _():
                 back_step(h, t)
 
-        @pl.when(s + 1 < nzh)
-        def _():
-            i = s + 1
-
-            arrive(i)
-            dispatch(i)
-
         done = s - lat
 
         @pl.when(done >= 0)
@@ -396,6 +403,11 @@
         @pl.when((done >= 1) & (which_of(done - 1) == 1))
         def _():
             combine(chunk_of(done - 1))
+            send_units(chunk_of(done - 1), 0, units // 2)
+
+        @pl.when((done >= 2) & (which_of(done - 2) == 1))
+        def _():
+            send_units(chunk_of(done - 2), units // 2, units)
 
         @pl.when((done >= 4) & (which_of(done - 4) == 1))
         def _():
@@ -409,7 +421,11 @@
 
     tiles = fe // tile
     finish_w_out(0, tiles // 2)
+    for t, (i, j) in enumerate(order):
+        if j == 1 and t == n_half - 2:
+            send_units(i, units // 2, units)
     combine(order[-1][0])
+    send_units(order[-1][0], 0, units)
     late = [i for t, (i, j) in enumerate(order) if j == 1 and t >= n_half - 4]
     for i in late[:-1]:
         sum_units(i)
@@ -429,7 +445,10 @@
         for i in range(1, nzh):
             total = total + zr[i, e].astype(F32)
         slot.append(jnp.concatenate([total[:CAP, :fh], total[CAP:, :fh]], axis=1))
-        gate_slot.append(total[:CAP, fh:] + total[CAP:, fh:])
+        gate = jnp.where(
+            lax.broadcasted_iota(jnp.int32, (CAP, LANES), 1) == me, total[:CAP, fh:] + total[CAP:, fh:], 0.0
+        )
+        gate_slot.append(jnp.broadcast_to(jnp.sum(gate, axis=1, keepdims=True), (CAP, LANES)))
     slot = jnp.concatenate(slot, axis=0)
     high = slot.astype(BF).astype(F32)
     middle = (slot - high).astype(BF).astype(F32)
@@ -442,11 +461,9 @@
 
     for i in range(1, nzh):
         wait_for(zs.at[i], zc_s.at[i])
-    for i in near:
-        wait_for(zbuf.at[0], z_s.at[i])
-    if far is not None:
+    for i in range(1, nzh):
         for e in range(WINDOW):
-            wait_for(zbuf.at[0, e], z_s.at[nzh + e])
+            wait_for(zbuf.at[i, e], z_s.at[i, e])
     for i in range(nzh):
         wait_for(rows.at[i, 0, pl.ds(0, units - 1)], xy_s.at[i])
         wait_for(rows.at[i, 0], sib_s.at[i])
@@ -507,7 +524,7 @@
             pltpu.VMEM((nzh, WINDOW, 2 * CAP, fe // 2 + LANES), BF),
             pltpu.VMEM((nzh, WINDOW, 2 * CAP, fe // 2 + LANES), BF),
             pltpu.VMEM((WINDOW, 2 * CAP, fe // 2 + LANES), F32),
-            dma((nzh + 2,)), dma((nzh + 2,)),
+            dma((nzh, WINDOW)), dma((nzh, WINDOW)),
             dma((nzh,)), dma((nzh,)),
             dma((nzh,)), dma((nzh,)),
             dma((2,)), dma((2, n_half)),

time: 99.9 us -> 98.7 us (0.988)
  no operation moved by 1% of the time
where the time goes in v3:
time: 98.7 us; the launch traced here: 98.6 us
  Pallas kernels  94.6 us (96%)
  local copies, waits for them, and re-layouts  3.31 us (3%)
    pallas_call x1, Pallas kernels, body(): pl.pallas_call(functools.partial(kernel, dims), out_shape=(pltpu.VMEM((to...  94.6 us
    unnamed x4, local copies, waits for them, and re-layouts  3.31 us

profile of v3, /device:TPU:1, one launch (start us, length us, event | category | flops | bytes accessed | tf_op | source)
XLA Modules:
  0.0 98.6 jit_solution(9283655864346338131)
XLA Ops:
  0.6 94.6 %shard_map.93 = (bf16[256,1024]{1,0:T(8,128)(2,1)S(1)}, f32[2,256]{1,0:T(2,128)S(1)}, f32[1024,256]{1,0:T(8,128)S(1)}, f32[256,1024]{1,0:T(8,128)S(1)}) custom-call(bf16[256,1024]{1,0:T(8,128)(2,1)} %tokens_hbm.1, bf16[256,1024]{1,0:T(8,128)(2,1)} %grad_out_hbm.1, s32[2,256]{1,0:T(2,128)} %bitcast.4, bf16[2,256]{1,0:T(2,128)(2,1)} %bitcast.5, ...), custom_call_target="tpu_custom_call" | custom-call | tf_op jit(solution)/shard_map/pallas_call | solution.py:495
  95.2 0.8 copy.14
  96.0 0.6 copy.15
  96.6 1.0 copy.16
  97.6 1.0 copy.17

commit v4 on v3

--- a/solution.py
+++ b/solution.py
@@ -13,7 +13,7 @@
 CAP = 8
 LANES = 128
 X_CHIPS, ZH_CHIPS = 4, 4
-HOP = 2
+HOP = 1
 OWN_LAST = False
 
 

time: 98.7 us -> 96.9 us (0.982)
  Pallas kernels: 94.6 us -> 92.8 us
    pallas_call x1, Pallas kernels: 94.6 us -> 92.8 us  [body(): pl.pallas_call(functools.partial(kernel, dims), out_shape=(pltpu.VMEM((to...]
where the time goes in v4:
time: 96.9 us; the launch traced here: 96.8 us
  Pallas kernels  92.8 us (96%)
  local copies, waits for them, and re-layouts  3.31 us (3%)
    pallas_call x1, Pallas kernels, body(): pl.pallas_call(functools.partial(kernel, dims), out_shape=(pltpu.VMEM((to...  92.8 us
    unnamed x4, local copies, waits for them, and re-layouts  3.31 us

profile of v4, /device:TPU:1, one launch (start us, length us, event | category | flops | bytes accessed | tf_op | source)
XLA Modules:
  0.0 96.8 jit_solution(6126212343279372090)
XLA Ops:
  0.6 92.8 %shard_map.93 = (bf16[256,1024]{1,0:T(8,128)(2,1)S(1)}, f32[2,256]{1,0:T(2,128)S(1)}, f32[1024,256]{1,0:T(8,128)S(1)}, f32[256,1024]{1,0:T(8,128)S(1)}) custom-call(bf16[256,1024]{1,0:T(8,128)(2,1)} %tokens_hbm.1, bf16[256,1024]{1,0:T(8,128)(2,1)} %grad_out_hbm.1, s32[2,256]{1,0:T(2,128)} %bitcast.4, bf16[2,256]{1,0:T(2,128)(2,1)} %bitcast.5, ...), custom_call_target="tpu_custom_call" | custom-call | tf_op jit(solution)/shard_map/pallas_call | solution.py:495
  93.4 0.8 copy.14
  94.2 0.6 copy.15
  94.8 1.0 %copy.16 = f32[1024,256]{1,0:T(8,128)} copy(f32[1024,256]{1,0:T(8,128)S(1)} %get-tuple-element.14) | data formatting | bytes 2097152
  95.8 1.0 %copy.17 = f32[256,1024]{1,0:T(8,128)} copy(f32[256,1024]{1,0:T(8,128)S(1)} %get-tuple-element.15) | data formatting | bytes 2097152
